TPU v7x, 32 devices: a whole 2x2x4 slice. The times are simulated.
32 devices in a mesh: engine: 4 (over x, core), fsdp: 4 (over z), tensor: 2 (over y).
Axes of the slice: x: 2, y: 2, z: 4, core: 2. Of those that a mesh axis runs over, the one named last changes fastest.
Arguments:
- layer_input: bfloat16 [2048, 16384], P(('engine', 'fsdp'), 'tensor'), may hold values from -6 to 6
- norm_gain: bfloat16 [16384], P('tensor'), may hold values from 0.099609375 to 1.8984375
- query_base: bfloat16 [16384, 256], P(('engine', 'fsdp'), 'tensor'), may hold values from -0.046875 to 0.046875
- query_down: bfloat16 [16384, 64], P(('engine', 'fsdp')), may hold values from -0.046875 to 0.046875
- query_up: bfloat16 [64, 256], P(None, 'tensor'), may hold values from -0.29882812 to 0.29882812
- kv_base: bfloat16 [2, 8192, 256], P('tensor', ('engine', 'fsdp')), may hold values from -0.046875 to 0.046875
- output_base_weight: bfloat16 [256, 2, 8192], P(None, 'tensor', ('engine', 'fsdp')), may hold values from -0.375 to 0.375
- output_down_factor: bfloat16 [256, 64], P('tensor'), may hold values from -0.375 to 0.375
- output_up_factor: bfloat16 [64, 2, 8192], P(None, 'tensor', ('engine', 'fsdp')), may hold values from -0.29882812 to 0.29882812
- cache_keys: bfloat16 [16, 512, 128], P(('engine', 'fsdp')), may hold values from -250 to 250
- cache_values: bfloat16 [16, 512, 128], P(('engine', 'fsdp')), may hold values from -6 to 6
- positions: int32 [16, 128], P(('engine', 'fsdp')), may hold values from 0 to 767, as said below
- offsets: int32 [16], P(('engine', 'fsdp')), may hold values from 0 to 512, as said below
Outputs:
- attended: bfloat16 [2048, 16384], P(('engine', 'fsdp'), 'tensor')
Inputs may be any that keep to these rules, and one draw needn't show every extreme that they name: `offsets`: each group's offset is its count of valid cache slots; some group has 512 and some group has 0. `positions`: positions rise along each group's row, by 1 or 2 a token; the first is its group's offset or one more; the group with 512 valid slots rises by 2 at every token.
All inputs are finite; a program needn't handle non-finite values.
Results may differ from a plain program's by a relative error of at most 0.03.
Values may be sent and summed in bfloat16 or wider, within the bound.
A program may use at most 64 MiB of HBM per device.

v0:
```python
import jax
import jax.numpy as jnp
from jax import lax
from jax.sharding import PartitionSpec as P


def rotate(values, places):
    half = values.shape[-1] // 2
    index = jnp.arange(half).astype(jnp.float32)
    inverse = jnp.exp(index * (-2.0 / values.shape[-1]) * jnp.log(jnp.float32(500000.0)))
    angle = places.astype(jnp.float32)[:, None] * inverse[None, :]
    cosine = jnp.cos(angle)
    sine = jnp.sin(angle)
    first = values[:, :half]
    second = values[:, half:]
    return jnp.concatenate([first * cosine - second * sine, second * cosine + first * sine], axis=1)


def attend(query, new_keys, new_values, old_keys, old_values, offset):
    tok_count = query.shape[0]
    slots = old_keys.shape[0]
    keys_all = jnp.concatenate([old_keys, new_keys], axis=0)
    values_all = jnp.concatenate([old_values, new_values], axis=0)
    scores = jnp.dot(query, keys_all.T, preferred_element_type=jnp.float32) * query.shape[-1] ** (
        -0.5
    )
    slot_seen = jnp.broadcast_to(jnp.arange(slots)[None, :] < offset, (tok_count, slots))
    rows = jnp.arange(tok_count)
    new_seen = rows[None, :] <= rows[:, None]
    seen = jnp.concatenate([slot_seen, new_seen], axis=1)
    scores = jnp.where(seen, scores, jnp.float32(-1e30))
    top = jnp.max(scores, axis=1, keepdims=True)
    probs = jnp.exp(scores - top)
    weights = (probs / jnp.sum(probs, axis=1, keepdims=True)).astype(jnp.bfloat16)
    return jnp.dot(weights, values_all, preferred_element_type=jnp.float32).astype(jnp.bfloat16)


def per_device(
    layer_input,
    norm_gain,
    query_base,
    query_down,
    query_up,
    kv_base,
    output_base_weight,
    output_down_factor,
    output_up_factor,
    cache_keys,
    cache_values,
    positions,
    offsets,
):
    head_size = query_base.shape[1]
    tok_count = layer_input.shape[0]
    full_input, full_gain, complete_down_factor = (
        lax.all_gather(layer_input, "tensor", axis=1, tiled=True),
        lax.all_gather(norm_gain, "tensor", axis=0, tiled=True),
        lax.all_gather(output_down_factor, "tensor", axis=0, tiled=True),
    )
    wide = full_input.astype(jnp.float32)
    scale = lax.rsqrt(jnp.mean(wide * wide, axis=1, keepdims=True) + 1e-05)
    normed = (wide * scale * full_gain.astype(jnp.float32)[None, :]).astype(jnp.bfloat16)
    local_normed = (
        layer_input.astype(jnp.float32) * scale * norm_gain.astype(jnp.float32)[None, :]
    ).astype(jnp.bfloat16)
    merged_query = (
        query_base.astype(jnp.float32)
        + 2.0 * jnp.dot(query_down, query_up, preferred_element_type=jnp.float32)
    ).astype(jnp.bfloat16)
    columns = normed
    query_raw = jnp.dot(
        columns,
        lax.all_gather(merged_query, ("engine", "fsdp"), axis=0, tiled=True),
        preferred_element_type=jnp.float32,
    )
    columns = local_normed
    kv_part = jnp.dot(
        columns,
        lax.all_gather(kv_base, ("engine", "fsdp"), axis=1, tiled=True)[0],
        preferred_element_type=jnp.float32,
    )
    kv_total = lax.psum(kv_part.astype(jnp.bfloat16), "tensor").astype(jnp.float32)
    places = positions[0]
    query = rotate(query_raw, places).astype(jnp.bfloat16)
    new_keys = rotate(kv_total[:, :head_size], places).astype(jnp.bfloat16)
    new_values = kv_total[:, head_size:].astype(jnp.bfloat16)
    head_out = attend(query, new_keys, new_values, cache_keys[0], cache_values[0], offsets[0])
    adapter_output_delta = jnp.einsum(
        "lz,zam->lam",
        complete_down_factor.astype(jnp.float32),
        output_up_factor.astype(jnp.float32),
    )
    combined_output_weight = (
        output_base_weight.astype(jnp.float32) + 2.0 * adapter_output_delta
    ).astype(jnp.bfloat16)
    own_rows = lax.all_to_all(
        combined_output_weight, "tensor", split_axis=0, concat_axis=1, tiled=True
    )
    terms = jnp.einsum(
        "tk,kbn->tbn",
        head_out,
        lax.all_gather(own_rows, ("engine", "fsdp"), axis=2, tiled=True),
        preferred_element_type=jnp.float32,
    )
    flat_terms = terms.reshape(tok_count, terms.shape[1] * terms.shape[2])
    attended = lax.psum_scatter(
        flat_terms.astype(jnp.bfloat16), "tensor", scatter_dimension=1, tiled=True
    )
    return attended


def solution(mesh):
    in_specs = (
        P(("engine", "fsdp"), "tensor"),
        P("tensor"),
        P(("engine", "fsdp"), "tensor"),
        P(("engine", "fsdp"), None),
        P(None, "tensor"),
        P("tensor", ("engine", "fsdp"), None),
        P(None, "tensor", ("engine", "fsdp")),
        P("tensor", None),
        P(None, "tensor", ("engine", "fsdp")),
        P(("engine", "fsdp"), None, None),
        P(("engine", "fsdp"), None, None),
        P(("engine", "fsdp"), None),
        P(("engine", "fsdp")),
    )
    out_specs = P(("engine", "fsdp"), "tensor")
    return jax.shard_map(
        per_device, mesh=mesh, in_specs=in_specs, out_specs=out_specs, check_vma=False
    )
```

profile of v0, /device:TPU:1, one launch (start us, length us, event | category | flops | bytes accessed | tf_op | source)
XLA Modules:
  0.0 327.0 jit_solution(10870656055782339650)
XLA Ops:
  6.5 0.7 all-gather.6.cloned.1.call-update
  7.3 0.7 all-gather.10.cloned.1.call-update
  8.1 1.9 fusion.16
  10.0 4.1 %all_gather.22 = bf16[256,64]{0,1:T(8,128)(2,1)S(1)} all-gather(bf16[128,64]{0,1:T(8,128)(2,1)} %param.20), channel_id=1, replica_groups=mesh['engine'=4,'fsdp'=4,'tensor'=2] {'tensor'}, dimensions={0}, use_global_device_ids=true | all-gather | bytes 49152 | tf_op jit(solution)/shard_map/all_gather | solution.py:58
  14.2 1.2 fusion.15
  15.9 0.8 reduce
  16.7 0.9 reshape.40
  17.6 3.5 %all-to-all-start = ((bf16[2,2,32768]{2,1,0:T(2,128)(2,1)}), bf16[2,2,32768]{2,1,0:T(2,128)(2,1)S(1)}, u32[]{:S(2)}, u32[]{:S(2)}) async-start(bf16[2,2,32768]{2,1,0:T(2,128)(2,1)} %reshape.40), calls=%async_computation | async-start | bytes 524288 | tf_op jit(solution)/shard_map/all_to_all | solution.py:96
  21.2 49.4 %all-gather.6.cloned.1.call-done = bf16[128,16384]{1,0:T(8,128)(2,1)} async-done(((bf16[128,8192]{1,0:T(8,128)(2,1)}), bf16[128,16384]{1,0:T(8,128)(2,1)}) %all-gather.6.cloned.1.call-update) | async-done | bytes 4194320 | tf_op jit(solution)/shard_map/all_gather | solution.py:56
  70.6 3.1 fusion
  73.7 50.3 %all-gather.10.cloned.1.call-done = bf16[1,8192,256]{2,1,0:T(8,128)(2,1)} async-done(((bf16[1,512,256]{2,1,0:T(8,128)(2,1)}), bf16[1,8192,256]{2,1,0:T(8,128)(2,1)}) %all-gather.10.cloned.1.call-update) | async-done | bytes 4194320 | tf_op jit(solution)/shard_map/all_gather | solution.py:79
  124.0 4.7 %fusion.18 = bf16[128,256]{0,1:T(8,128)(2,1)} fusion(bf16[1,8192,256]{2,1,0:T(8,128)(2,1)} %all-gather.10.cloned.1.call-done, bf16[128,8192]{1,0:T(8,128)(2,1)S(1)} %copy-done.1, f32[8192]{0:T(1024)S(1)} %convert_element_type.81, f32[128]{0:T(128)S(1)} %add_rsqrt_fusion), kind=kOutput, calls=%fused_computation.24 | convolution fusion | flops 541097984 | bytes 6390272 | tf_op jit(solution)/shard_map/dot_general | solution.py:77
  129.0 0.7 copy.35
  129.9 3.3 all_gather.19
  133.9 41.4 %all-gather.8.cloned.1.call-done = bf16[16384,128]{1,0:T(8,128)(2,1)} async-done(((bf16[1024,128]{1,0:T(8,128)(2,1)}), bf16[16384,128]{1,0:T(8,128)(2,1)}) %all-gather.8.cloned.1.call-update) | async-done | bytes 4194320 | tf_op jit(solution)/shard_map/all_gather | solution.py:73
  175.3 5.5 %fusion.3 = f32[128,128]{0,1:T(8,128)S(1)} fusion(bf16[16384,128]{1,0:T(8,128)(2,1)} %all-gather.8.cloned.1.call-done, bf16[128,16384]{1,0:T(8,128)(2,1)} %all-gather.6.cloned.1.call-done, f32[16384]{0:T(1024)S(1)} %convert_element_type.73, f32[128]{0:T(128)S(1)} %add_rsqrt_fusion), kind=kOutput, calls=%fused_computation.6 | convolution fusion | flops 545259520 | bytes 8520192 | tf_op jit(solution)/shard_map/dot_general | solution.py:71
  180.8 15.1 %all-reduce.2.cloned.1.call-done = bf16[128,256]{0,1:T(8,128)(2,1)} async-done(((bf16[128,256]{0,1:T(8,128)(2,1)}), bf16[128,256]{0,1:T(8,128)(2,1)}) %all-reduce.2.cloned.1.call-update) | async-done | bytes 65552 | tf_op jit(solution)/shard_map/psum | solution.py:82
  195.8 0.8 convert_element_type.84
  197.0 0.8 slice.28
  198.5 53.4 %all-gather.12.cloned.1.call-done = bf16[128,2,1,8192]{3,0,1,2:T(8,128)(2,1)} async-done(((bf16[128,2,1,512]{3,0,1,2:T(8,128)(2,1)}), bf16[128,2,1,8192]{3,0,1,2:T(8,128)(2,1)}) %all-gather.12.cloned.1.call-update) | async-done | bytes 4194320 | tf_op jit(solution)/shard_map/all_gather | solution.py:102
  251.8 5.6 %convolution_convert_fusion = bf16[128,2,8192]{2,0,1:T(8,128)(2,1)} fusion(bf16[128,2,1,8192]{3,0,1,2:T(8,128)(2,1)} %all-gather.12.cloned.1.call-done, f32[128,640]{1,0:T(8,128)S(1)} %get-tuple-element.12, bf16[128,128]{1,0:T(8,128)(2,1)S(1)} %copy.30, bf16[512,128]{1,0:T(8,128)(2,1)S(1)} %bitcast.37, f32[128]{0:T(128)S(1)} %fusion.22, ...), kind=kOutput, calls=%fused_computation.2 | convolution fusion | flops 560529408 | bytes 8881152 | tf_op jit(solution)/shard_map/tk,kbn->tbn/dot_general | solution.py:99
  257.5 6.4 %copy.32 = bf16[128,2,8192]{0,2,1:T(8,128)(2,1)} copy(bf16[128,2,8192]{2,0,1:T(8,128)(2,1)} %convolution_convert_fusion) | data formatting | bytes 8388608 | tf_op jit(solution)/shard_map/convert_element_type | solution.py:107
  263.9 52.2 %reduce-scatter.2.cloned.1.call-done = bf16[128,8192]{0,1:T(8,128)(2,1)} async-done(((bf16[128,16384]{0,1:T(8,128)(2,1)}), bf16[128,8192]{0,1:T(8,128)(2,1)}) %reduce-scatter.2.cloned.1.call-update) | async-done | bytes 2097168 | tf_op jit(solution)/shard_map/reduce_scatter | solution.py:106
  316.1 4.1 %copy.33 = bf16[128,8192]{1,0:T(8,128)(2,1)} copy(bf16[128,8192]{0,1:T(8,128)(2,1)} %reduce-scatter.2.cloned.1.call-done) | data formatting | bytes 4194304 | tf_op jit(solution)/shard_map/reduce_scatter | solution.py:106
  (39 shorter events, 2.1 us)
Async XLA Ops:
  6.5 1.5 copy-start
  6.5 14.6 %copy-start.3 = (bf16[8192]{0:T(1024)(128)(2,1)S(1)}, bf16[8192]{0:T(1024)(128)(2,1)}, u32[]{:S(2)}) copy-start(bf16[8192]{0:T(1024)(128)(2,1)} %param.14) | copy-start | bytes 49156
  6.5 64.0 %all-gather.6.cloned.1.call-start = ((), (), s32[]{:S(2)}) async-start(), calls=%async_computation.2 | async-start | bytes 6291456 | tf_op jit(solution)/shard_map/all_gather | solution.py:56
  7.3 116.7 %copy-start.1 = (bf16[128,8192]{1,0:T(8,128)(2,1)S(1)}, bf16[128,8192]{1,0:T(8,128)(2,1)}, u32[]{:S(2)}) copy-start(bf16[128,8192]{1,0:T(8,128)(2,1)} %param.13) | copy-start | bytes 6291460
  7.3 116.7 %all-gather.10.cloned.1.call-start = ((), (), s32[]{:S(2)}) async-start(), calls=%async_computation.4 | async-start | bytes 4456448 | tf_op jit(solution)/shard_map/all_gather | solution.py:79
  8.0 167.2 %all-gather.8.cloned.1.call-start = ((), (), s32[]{:S(2)}) async-start(), calls=%async_computation.3 | async-start | bytes 4456448 | tf_op jit(solution)/shard_map/all_gather | solution.py:73
  17.6 111.1 %all-to-all-start = ((bf16[2,2,32768]{2,1,0:T(2,128)(2,1)}), bf16[2,2,32768]{2,1,0:T(2,128)(2,1)S(1)}, u32[]{:S(2)}, u32[]{:S(2)}) async-start(bf16[2,2,32768]{2,1,0:T(2,128)(2,1)} %reshape.40), calls=%async_computation | async-start | bytes 524288 | tf_op jit(solution)/shard_map/all_to_all | solution.py:96
  21.1 174.7 %all-reduce.2.cloned.1.call-start = ((), (), s32[]{:S(2)}) async-start(), calls=%async_computation.5 | async-start | bytes 131072 | tf_op jit(solution)/shard_map/psum | solution.py:82
  73.7 60.2 %copy-start.5 = (s32[1,128]{1,0:T(1,128)S(1)}, s32[1,128]{1,0:T(1,128)}, u32[]{:S(2)}) copy-start(s32[1,128]{1,0:T(1,128)} %param.24) | copy-start | bytes 1540
  128.7 123.1 %all-gather.12.cloned.1.call-start = ((), (), s32[]{:S(2)}) async-start(), calls=%async_computation.7 | async-start | bytes 4456448 | tf_op jit(solution)/shard_map/all_gather | solution.py:102
  129.8 186.3 %reduce-scatter.2.cloned.1.call-start = ((), (), s32[]{:S(2)}) async-start(), calls=%async_computation.6 | async-start | bytes 6291456 | tf_op jit(solution)/shard_map/reduce_scatter | solution.py:106
  133.9 64.0 %copy-start.4 = (bf16[1,512,128]{2,1,0:T(8,128)(2,1)S(1)}, bf16[1,512,128]{2,1,0:T(8,128)(2,1)}, u32[]{:S(2)}) copy-start(bf16[1,512,128]{2,1,0:T(8,128)(2,1)} %param.22) | copy-start | bytes 393220
  133.9 118.0 %copy-start.2 = (bf16[1,512,128]{2,1,0:T(8,128)(2,1)S(1)}, bf16[1,512,128]{2,1,0:T(8,128)(2,1)}, u32[]{:S(2)}) copy-start(bf16[1,512,128]{2,1,0:T(8,128)(2,1)} %param.23) | copy-start | bytes 393220
Sparse Core Ops, SparseCore 0:
  8.9 61.6 all-gather.5
  72.8 51.1 all-gather.9
  126.2 49.0 all-gather.7
  177.3 18.4 all-reduce.1
  197.7 54.0 all-gather.11
  264.0 52.0 reduce-scatter.1
where the time goes:
time: 328 us; the launch traced here: 327 us
  waiting for transfers between devices  263 us (80%)
  matrix products  19.3 us (6%)
  between operations  14.3 us (4%)
  local copies, waits for them, and re-layouts  13.9 us (4%)
  blocking collectives  7.42 us (2%)
  other arithmetic  5.2 us (2%)
  starting transfers between devices  3.69 us (1%)
    all_gather x1, waiting for transfers between devices, per_device(): lax.all_gather(own_rows, ('engine', 'fsdp'), axis=2, tiled=True)  53.4 us
    reduce_scatter x1, waiting for transfers between devices, per_device(): lax.psum_scatter(flat_terms.astype(jnp.bfloat16), 'tensor', scatter_dimen...  52.2 us
    all_gather x1, waiting for transfers between devices, per_device(): lax.all_gather(kv_base, ('engine', 'fsdp'), axis=1, tiled=True)[0]  50.3 us
    all_gather x1, waiting for transfers between devices, per_device(): lax.all_gather(layer_input, 'tensor', axis=1, tiled=True)  49.4 us
    all_gather x1, waiting for transfers between devices, per_device(): lax.all_gather(merged_query, ('engine', 'fsdp'), axis=0, tiled=True)  41.4 us
    psum x1, waiting for transfers between devices, per_device(): lax.psum(kv_part.astype(jnp.bfloat16), 'tensor').astype(jnp.float32)  15.1 us
  transfers between devices with their start and end apart: 7, of which 6 were waited for; matrix products, arithmetic and copies ran while one was open for 7% of the time, Pallas kernels for 0%

commit v1 on v0

--- a/solution.py
+++ b/solution.py
@@ -1,7 +1,15 @@
+import functools
+
 import jax
 import jax.numpy as jnp
 from jax import lax
+from jax.experimental import pallas as pl
+from jax.experimental.pallas import tpu as pltpu
 from jax.sharding import PartitionSpec as P
+
+MESH = pl.DeviceIdType.MESH
+KV, QUERY, OUT = 0, 1, 2
+SIB, CROSS, LEFT, RIGHT = 0, 1, 2, 3
 
 
 def rotate(values, places):
@@ -35,7 +43,7 @@
     return jnp.dot(weights, values_all, preferred_element_type=jnp.float32).astype(jnp.bfloat16)
 
 
-def per_device(
+def per_device_plain(
     layer_input,
     norm_gain,
     query_base,
@@ -109,6 +117,442 @@
     return attended
 
 
+def kernel(
+    n_f,
+    input_ref,
+    gain_ref,
+    qbase_ref,
+    qdown_ref,
+    qup_ref,
+    kvbase_ref,
+    obase_ref,
+    odown_ref,
+    oup_ref,
+    ckeys_ref,
+    cvalues_ref,
+    places_ref,
+    offset_ref,
+    result_ref,
+    kv_buf,
+    q_buf,
+    o_buf,
+    normed,
+    squares,
+    down_full,
+    kv_part,
+    q_total,
+    heads,
+    recv_sem,
+    send_sem,
+    y_recv,
+    y_send,
+    n_recv,
+    n_send,
+):
+    engine = lax.axis_index("engine")
+    z = lax.axis_index("fsdp")
+    t = lax.axis_index("tensor")
+    core = lax.rem(engine, 2)
+    sibling = engine + 1 - 2 * core
+    across = lax.rem(engine + 2, 4)
+    other = 1 - t
+    bufs = (kv_buf, q_buf, o_buf)
+    groups = 4 * n_f
+    tok = input_ref.shape[0]
+    head = qbase_ref.shape[1]
+    piece = kvbase_ref.shape[0]
+    half_groups = groups // 2
+    rank = odown_ref.shape[1]
+    width = 2 * input_ref.shape[1]
+
+    def copy(m, g, way):
+        target = {
+            SIB: (sibling, z, t),
+            CROSS: (across, z, t),
+            LEFT: (engine, jnp.maximum(z - 1, 0), t),
+            RIGHT: (engine, jnp.minimum(z + 1, n_f - 1), t),
+        }[way]
+        return pltpu.make_async_remote_copy(
+            src_ref=bufs[m].at[g],
+            dst_ref=bufs[m].at[g],
+            send_sem=send_sem.at[m, way, g],
+            recv_sem=recv_sem.at[m, g],
+            device_id=target,
+            device_id_type=MESH,
+        )
+
+    def to_partner(ref, k):
+        return pltpu.make_async_remote_copy(
+            src_ref=ref.at[t],
+            dst_ref=ref.at[t],
+            send_sem=y_send.at[k],
+            recv_sem=y_recv.at[k],
+            device_id=(engine, z, other),
+            device_id_type=MESH,
+        )
+
+    def from_partner(ref, k):
+        return pltpu.make_async_remote_copy(
+            src_ref=ref.at[other],
+            dst_ref=ref.at[other],
+            send_sem=y_send.at[k],
+            recv_sem=y_recv.at[k],
+            device_id=(engine, z, other),
+            device_id_type=MESH,
+        )
+
+    def normed_copy(side, k):
+        rows = normed.at[pl.ds(side * groups + 2 * k, 2)]
+        return pltpu.make_async_remote_copy(
+            src_ref=rows,
+            dst_ref=rows,
+            send_sem=n_send.at[k],
+            recv_sem=n_recv.at[k],
+            device_id=(engine, z, other),
+            device_id_type=MESH,
+        )
+
+    def own(m):
+        g = engine * n_f + z
+        copy(m, g, CROSS).start()
+
+        @pl.when(z > 0)
+        def _():
+            copy(m, g, LEFT).start()
+
+        @pl.when(z < n_f - 1)
+        def _():
+            copy(m, g, RIGHT).start()
+
+        copy(m, g, SIB).start()
+
+    def along(m, d):
+        @pl.when(z >= d)
+        def _():
+            g = engine * n_f + z - d
+            copy(m, g, SIB).wait_recv()
+
+            @pl.when(z < n_f - 1)
+            def _():
+                copy(m, g, RIGHT).start()
+
+            copy(m, g, CROSS).start()
+            copy(m, g, SIB).start()
+
+        @pl.when(z + d < n_f)
+        def _():
+            g = engine * n_f + z + d
+            copy(m, g, SIB).wait_recv()
+
+            @pl.when(z > 0)
+            def _():
+                copy(m, g, LEFT).start()
+
+            copy(m, g, CROSS).start()
+            copy(m, g, SIB).start()
+
+    def crossing(m, d):
+        def take(zz):
+            g = across * n_f + zz
+            copy(m, g, SIB).wait_recv()
+            copy(m, g, SIB).start()
+
+        if d == 0:
+            take(z)
+        else:
+            pl.when(z >= d)(lambda: take(z - d))
+            pl.when(z + d < n_f)(lambda: take(z + d))
+
+    def from_sibling(m):
+        def both(k, carry):
+            copy(m, sibling * n_f + k, SIB).wait_recv()
+            copy(m, lax.rem(sibling + 2, 4) * n_f + k, SIB).wait_recv()
+            return carry
+
+        lax.fori_loop(0, n_f, both, 0)
+
+    barrier = pltpu.get_barrier_semaphore()
+
+    def greet(target):
+        pl.semaphore_signal(barrier, inc=1, device_id=target, device_id_type=MESH)
+
+    greet((sibling, z, t))
+    greet((across, z, t))
+    greet((engine, z, other))
+    pl.when(z > 0)(lambda: greet((engine, z - 1, t)))
+    pl.when(z < n_f - 1)(lambda: greet((engine, z + 1, t)))
+
+    mine = engine * n_f + z
+    kv_buf[mine] = kvbase_ref[...]
+    total = jnp.zeros((tok, 128), jnp.float32)
+    for k in range(input_ref.shape[1] // 128):
+        wide = input_ref[:, k * 128 : (k + 1) * 128].astype(jnp.float32)
+        total = total + wide * wide
+    squares[t] = total
+    down_full[t] = jnp.zeros(down_full.shape[1:], jnp.bfloat16)
+    down_full[t, :, :rank] = odown_ref[...]
+
+    pl.semaphore_wait(barrier, 5 - (z == 0).astype(jnp.int32) - (z == n_f - 1).astype(jnp.int32))
+
+    own(KV)
+    to_partner(squares, 0).start()
+    to_partner(down_full, 1).start()
+    q_buf[mine] = (
+        qbase_ref[...].astype(jnp.float32)
+        + 2.0 * jnp.dot(qdown_ref[...], qup_ref[...], preferred_element_type=jnp.float32)
+    ).astype(jnp.bfloat16)
+
+    from_partner(squares, 0).wait_recv()
+    mean = jnp.sum(squares[0] + squares[1], axis=1, keepdims=True) * (1.0 / width)
+    scale = lax.rsqrt(mean + 1e-05)
+    for k in range(groups):
+        cut = slice(k * piece, (k + 1) * piece)
+        normed[t * groups + k] = (
+            input_ref[:, cut].astype(jnp.float32) * scale * gain_ref[:, cut].astype(jnp.float32)
+        ).astype(jnp.bfloat16)
+        if k % 2 == 1:
+            normed_copy(t, k // 2).start()
+
+    along(KV, 1)
+    own(QUERY)
+    crossing(KV, 0)
+    along(KV, 2)
+
+    from_partner(down_full, 1).wait_recv()
+    for side in range(2):
+        rows = slice(side * head, (side + 1) * head)
+        o_buf[mine, rows, :] = (
+            obase_ref[rows, :].astype(jnp.float32)
+            + 2.0
+            * jnp.dot(
+                down_full[side, :, :rank], oup_ref[...], preferred_element_type=jnp.float32
+            )
+        ).astype(jnp.bfloat16)
+
+    crossing(KV, 1)
+    along(KV, 3)
+    crossing(KV, 2)
+    along(QUERY, 1)
+    crossing(KV, 3)
+    own(OUT)
+    crossing(QUERY, 0)
+    along(QUERY, 2)
+
+    from_sibling(KV)
+    kv_part[t] = jnp.zeros(kv_part.shape[1:], jnp.float32)
+
+    def kv_step(g, carry):
+        kv_part[t] += jnp.dot(
+            normed[t * groups + g], kv_buf[g], preferred_element_type=jnp.float32
+        )
+        return carry
+
+    lax.fori_loop(0, groups // 2, kv_step, 0)
+    crossing(QUERY, 1)
+    along(QUERY, 3)
+    lax.fori_loop(groups // 2, groups, kv_step, 0)
+    to_partner(kv_part, 2).start()
+    along(OUT, 1)
+    crossing(QUERY, 2)
+    crossing(QUERY, 3)
+
+    lane = lax.broadcasted_iota(jnp.int32, (tok, head), 1)
+    low = lane < head // 2
+    index = jnp.where(low, lane, lane - head // 2).astype(jnp.float32)
+    inverse = jnp.exp(index * (-2.0 / head) * jnp.log(jnp.full((tok, head), 500000.0, jnp.float32)))
+    places = jnp.broadcast_to(places_ref[...].astype(jnp.float32), (head, tok)).T
+    angle = places * inverse
+    cosine = jnp.cos(angle)
+    sine = jnp.where(low, -jnp.sin(angle), jnp.sin(angle))
+
+    def rope(values):
+        return values * cosine + pltpu.roll(values, head // 2, 1) * sine
+
+    from_sibling(QUERY)
+    q_total[...] = jnp.zeros_like(q_total)
+
+    def q_step(g):
+        q_total[...] += jnp.dot(
+            normed[2 * g], q_buf[g, :piece, :], preferred_element_type=jnp.float32
+        ) + jnp.dot(normed[2 * g + 1], q_buf[g, piece:, :], preferred_element_type=jnp.float32)
+
+    def q_near(k, carry):
+        q_step(t * half_groups + k)
+        return carry
+
+    def q_far(k, carry):
+        normed_copy(other, k).wait_recv()
+        q_step(other * half_groups + k)
+        return carry
+
+    lax.fori_loop(0, half_groups, q_near, 0)
+    crossing(OUT, 0)
+    along(OUT, 2)
+    lax.fori_loop(0, half_groups, q_far, 0)
+
+    query = rope(q_total[...]).astype(jnp.bfloat16)
+    from_partner(kv_part, 2).wait_recv()
+    kv = kv_part[0] + kv_part[1]
+    new_keys = rope(kv[:, :head]).astype(jnp.bfloat16)
+    new_values = kv[:, head:].astype(jnp.bfloat16)
+    dims = (((1,), (1,)), ((), ()))
+    slots = ckeys_ref.shape[0]
+    factor = head ** (-0.5)
+    old = lax.dot_general(query, ckeys_ref[...], dims, preferred_element_type=jnp.float32) * factor
+    new = lax.dot_general(query, new_keys, dims, preferred_element_type=jnp.float32) * factor
+    seen = lax.broadcasted_iota(jnp.int32, (tok, slots), 1) < offset_ref[0]
+    rows = lax.broadcasted_iota(jnp.int32, (tok, tok), 0)
+    columns = lax.broadcasted_iota(jnp.int32, (tok, tok), 1)
+    old = jnp.where(seen, old, jnp.float32(-1e30))
+    new = jnp.where(columns <= rows, new, jnp.float32(-1e30))
+    top = jnp.maximum(
+        jnp.max(old, axis=1, keepdims=True), jnp.max(new, axis=1, keepdims=True)
+    )
+    old = jnp.exp(old - top)
+    new = jnp.exp(new - top)
+    summed = jnp.sum(old, axis=1, keepdims=True) + jnp.sum(new, axis=1, keepdims=True)
+    old = (old / summed).astype(jnp.bfloat16)
+    new = (new / summed).astype(jnp.bfloat16)
+    heads[t] = (
+        jnp.dot(old, cvalues_ref[...], preferred_element_type=jnp.float32)
+        + jnp.dot(new, new_values, preferred_element_type=jnp.float32)
+    ).astype(jnp.bfloat16)
+    to_partner(heads, 3).start()
+    along(OUT, 3)
+    from_partner(heads, 3).wait_recv()
+
+    def project(g):
+        first = jnp.dot(heads[0], o_buf[g, :head, :], preferred_element_type=jnp.float32)
+        second = jnp.dot(heads[1], o_buf[g, head:, :], preferred_element_type=jnp.float32)
+        both = first.astype(jnp.bfloat16).astype(jnp.float32) + second.astype(
+            jnp.bfloat16
+        ).astype(jnp.float32)
+        result_ref[:, pl.ds(pl.multiple_of(g * piece, piece), piece)] = both.astype(jnp.bfloat16)
+
+    def column(which):
+        def step(k, carry):
+            project(which * n_f + k)
+            return carry
+
+        lax.fori_loop(0, n_f, step, 0)
+
+    crossing(OUT, 1)
+    column(engine)
+    crossing(OUT, 2)
+    crossing(OUT, 3)
+    column(across)
+
+    def sibling_column(which):
+        def step(k, carry):
+            g = which * n_f + k
+            copy(OUT, g, SIB).wait_recv()
+            project(g)
+            return carry
+
+        lax.fori_loop(0, n_f, step, 0)
+
+    sibling_column(sibling)
+    sibling_column(lax.rem(sibling + 2, 4))
+
+    for m in range(3):
+
+        def drain(k, carry, m=m):
+            g = engine * n_f + k
+            copy(m, g, SIB).wait_send()
+            copy(m, g, CROSS).wait_send()
+            copy(m, across * n_f + k, SIB).wait_send()
+
+            @pl.when((z > 0) & (k >= z))
+            def _():
+                copy(m, g, LEFT).wait_send()
+
+            @pl.when((z < n_f - 1) & (k <= z))
+            def _():
+                copy(m, g, RIGHT).wait_send()
+
+            return carry
+
+        lax.fori_loop(0, n_f, drain, 0)
+
+    def drain_normed(k, carry):
+        normed_copy(t, k).wait_send()
+        return carry
+
+    lax.fori_loop(0, half_groups, drain_normed, 0)
+    to_partner(squares, 0).wait_send()
+    to_partner(down_full, 1).wait_send()
+    to_partner(kv_part, 2).wait_send()
+    to_partner(heads, 3).wait_send()
+
+
+def per_device(
+    n_f,
+    layer_input,
+    norm_gain,
+    query_base,
+    query_down,
+    query_up,
+    kv_base,
+    output_base_weight,
+    output_down_factor,
+    output_up_factor,
+    cache_keys,
+    cache_values,
+    positions,
+    offsets,
+):
+    tok, features = layer_input.shape
+    depth, head = query_base.shape
+    groups = 4 * n_f
+    kv_base = kv_base[0]
+    output_base_weight = output_base_weight[:, 0]
+    output_up_factor = output_up_factor[:, 0]
+    piece = kv_base.shape[0]
+    vmem = pl.BlockSpec(memory_space=pltpu.VMEM)
+    smem = pl.BlockSpec(memory_space=pltpu.SMEM)
+    dma = pltpu.SemaphoreType.DMA
+    return pl.pallas_call(
+        functools.partial(kernel, n_f),
+        out_shape=jax.ShapeDtypeStruct((tok, features), jnp.bfloat16),
+        in_specs=[vmem] * 12 + [smem],
+        out_specs=vmem,
+        scratch_shapes=[
+            pltpu.VMEM((groups,) + kv_base.shape, jnp.bfloat16),
+            pltpu.VMEM((groups,) + query_base.shape, jnp.bfloat16),
+            pltpu.VMEM((groups,) + output_base_weight.shape, jnp.bfloat16),
+            pltpu.VMEM((2 * groups, tok, piece), jnp.bfloat16),
+            pltpu.VMEM((2, tok, 128), jnp.float32),
+            pltpu.VMEM((2, head, 128), jnp.bfloat16),
+            pltpu.VMEM((2, tok, 2 * head), jnp.float32),
+            pltpu.VMEM((tok, head), jnp.float32),
+            pltpu.VMEM((2, tok, head), jnp.bfloat16),
+            dma((3, groups)),
+            dma((3, 4, groups)),
+            dma((4,)),
+            dma((4,)),
+            dma((groups // 2,)),
+            dma((groups // 2,)),
+        ],
+        compiler_params=pltpu.CompilerParams(
+            collective_id=0, has_side_effects=True, vmem_limit_bytes=48 * 1024 * 1024
+        ),
+    )(
+        layer_input,
+        norm_gain[None, :],
+        query_base,
+        query_down,
+        query_up,
+        kv_base,
+        output_base_weight,
+        output_down_factor,
+        output_up_factor,
+        cache_keys[0],
+        cache_values[0],
+        positions,
+        offsets,
+    )
+
+
 def solution(mesh):
     in_specs = (
         P(("engine", "fsdp"), "tensor"),
@@ -126,6 +570,9 @@
         P(("engine", "fsdp")),
     )
     out_specs = P(("engine", "fsdp"), "tensor")
+    shape = dict(mesh.shape)
+    paired = shape["tensor"] == 2 and shape["engine"] == 4
+    body = functools.partial(per_device, shape["fsdp"]) if paired else per_device_plain
     return jax.shard_map(
-        per_device, mesh=mesh, in_specs=in_specs, out_specs=out_specs, check_vma=False
-    )
+        body, mesh=mesh, in_specs=in_specs, out_specs=out_specs, check_vma=False
+    )

time: 328 us -> 96 us (0.29)
  waiting for transfers between devices: 263 us -> 0 us
  Pallas kernels: 0 us -> 81.8 us
  matrix products: 19.3 us -> 0 us
  between operations: 14.3 us -> 0.69 us
  blocking collectives: 7.42 us -> 0 us
  other arithmetic: 5.2 us -> 0 us
  starting transfers between devices: 3.69 us -> 0 us
    all_gather x4 -> x0, waiting for transfers between devices: 194 us -> none  [the longest x1 53.4 us: per_device(): lax.all_gather(own_rows, ('engine', 'fsdp'), axis=2, tiled=True)]
    pallas_call x0 -> x1, Pallas kernels: none -> 81.8 us  [per_device(): pl.pallas_call(functools.partial(kernel, n_f), out_shape=jax.ShapeDtypeSt...]
    reduce_scatter x1 -> x0, waiting for transfers between devices: 52.2 us -> none  [per_device(): lax.psum_scatter(flat_terms.astype(jnp.bfloat16), 'tensor', scatter_dimen...]
    dot_general x6 -> x0, matrix products: 19.3 us -> none  [the longest x1 5.64 us: per_device(): jnp.einsum('tk,kbn->tbn', head_out, lax.all_gather(own_rows, ('engine', '...]
    psum x1 -> x0, waiting for transfers between devices: 15.1 us -> none  [per_device(): lax.psum(kv_part.astype(jnp.bfloat16), 'tensor').astype(jnp.float32)]
    unnamed x15 -> x21, local copies, waits for them, and re-layouts: 1.94 us -> 11.7 us
    all_gather x2 -> x0, blocking collectives: 7.42 us -> none  [the longest x1 4.15 us: per_device(): lax.all_gather(output_down_factor, 'tensor', axis=0, tiled=True)]
    convert_element_type x2 -> x0, local copies, waits for them, and re-layouts: 6.9 us -> none  [the longest x1 6.38 us: per_device(): flat_terms.astype(jnp.bfloat16)]
  transfers between devices with their start and end apart: 7 -> 0, of which waited for: 6 -> 0; matrix products, arithmetic and copies ran while one was open for 7% -> 0% of each run, Pallas kernels for 0% -> 0%
where the time goes in v1:
time: 96 us; the launch traced here: 94.9 us
  Pallas kernels  81.8 us (85%)
  local copies, waits for them, and re-layouts  12.4 us (13%)
    pallas_call x1, Pallas kernels, per_device(): pl.pallas_call(functools.partial(kernel, n_f), out_shape=jax.ShapeDtypeSt...  81.8 us
    unnamed x21, local copies, waits for them, and re-layouts  11.7 us

profile of v1, /device:TPU:1, one launch (start us, length us, event | category | flops | bytes accessed | tf_op | source)
XLA Modules:
  0.0 94.9 jit_solution(15587783147095062907)
XLA Ops:
  0.7 0.7 broadcast_in_dim.3.gain_ref
  1.4 0.8 copy.15.odown_ref
  2.2 1.1 %copy.14.qdown_ref = bf16[1024,64]{1,0:T(8,128)(2,1)S(1)} copy(bf16[1024,64]{0,1:T(8,128)(2,1)} %param.16) | data formatting | bytes 262144 | tf_op args[3]
  3.3 0.0 copy-start
  3.3 1.6 %copy-done = bf16[128,8192]{1,0:T(8,128)(2,1)S(1)} copy-done((bf16[128,8192]{1,0:T(8,128)(2,1)S(1)}, bf16[128,8192]{1,0:T(8,128)(2,1)}, u32[]{:S(2)}) %copy-start) | copy-done | bytes 2097176
  4.9 0.0 copy-start.1
  4.9 0.9 copy-done.1
  5.9 0.0 copy-start.2
  5.9 0.9 copy-done.2
  6.8 0.0 copy-start.3
  6.8 0.9 copy-done.3
  7.8 0.0 copy-start.4
  7.8 0.9 copy-done.4
  8.7 0.0 copy-start.5
  8.7 0.9 copy-done.5
  9.6 0.0 copy-start.6
  9.6 0.8 copy-done.6
  10.4 0.0 copy-start.7
  10.4 0.7 copy-done.7
  11.1 0.0 copy-start.8
  11.1 0.7 copy-done.8
  11.8 81.8 %shard_map.127 = bf16[128,8192]{1,0:T(8,128)(2,1)S(1)} custom-call(bf16[128,8192]{1,0:T(8,128)(2,1)S(1)} %copy-done, bf16[1,8192]{1,0:T(2,128)(2,1)S(1)} %broadcast_in_dim.3.gain_ref, bf16[1024,128]{1,0:T(8,128)(2,1)S(1)} %copy-done.1, bf16[1024,64]{1,0:T(8,128)(2,1)S(1)} %copy.14.qdown_ref, bf16[64,128]{1,0:T(8,128)(2,1)S(1)} %copy-done.7, ...), custom_call_target="tpu_custom_call" | custom-call | tf_op jit(solution)/shard_map/pallas_call | solution.py:514
  93.6 1.3 %copy.18 = bf16[128,8192]{1,0:T(8,128)(2,1)} copy(bf16[128,8192]{1,0:T(8,128)(2,1)S(1)} %shard_map.127) | data formatting | bytes 4194304
Async XLA Ops:
  3.3 1.6 %copy-start = (bf16[128,8192]{1,0:T(8,128)(2,1)S(1)}, bf16[128,8192]{1,0:T(8,128)(2,1)}, u32[]{:S(2)}) copy-start(bf16[128,8192]{1,0:T(8,128)(2,1)} %input_ref.1) | copy-start | bytes 6291460
  4.9 0.9 %copy-start.1 = (bf16[1024,128]{1,0:T(8,128)(2,1)S(1)}, bf16[1024,128]{1,0:T(8,128)(2,1)}, u32[]{:S(2)}) copy-start(bf16[1024,128]{1,0:T(8,128)(2,1)} %qbase_ref.1) | copy-start | bytes 786436
  5.9 0.9 %copy-start.2 = (bf16[1,512,256]{2,1,0:T(8,128)(2,1)S(1)}, bf16[1,512,256]{2,1,0:T(8,128)(2,1)}, u32[]{:S(2)}) copy-start(bf16[1,512,256]{2,1,0:T(8,128)(2,1)} %param.18) | copy-start | bytes 786436
  6.8 0.9 %copy-start.3 = (bf16[256,1,512]{2,0,1:T(8,128)(2,1)S(1)}, bf16[256,1,512]{2,0,1:T(8,128)(2,1)}, u32[]{:S(2)}) copy-start(bf16[256,1,512]{2,0,1:T(8,128)(2,1)} %param.19) | copy-start | bytes 786436
  7.8 0.9 copy-start.4
  8.7 0.9 copy-start.5
  9.6 0.8 copy-start.6
  10.4 0.7 copy-start.7
  11.1 0.7 copy-start.8

commit v2 on v1

--- a/solution.py
+++ b/solution.py
@@ -119,20 +119,31 @@
 
 def kernel(
     n_f,
+    input_hbm,
+    gain_hbm,
+    qbase_hbm,
+    qdown_hbm,
+    qup_hbm,
+    kvbase_hbm,
+    obase_hbm,
+    odown_hbm,
+    oup_hbm,
+    ckeys_hbm,
+    cvalues_hbm,
+    places_hbm,
+    offset_ref,
+    result_ref,
     input_ref,
     gain_ref,
     qbase_ref,
     qdown_ref,
     qup_ref,
-    kvbase_ref,
     obase_ref,
     odown_ref,
     oup_ref,
     ckeys_ref,
     cvalues_ref,
     places_ref,
-    offset_ref,
-    result_ref,
     kv_buf,
     q_buf,
     o_buf,
@@ -142,12 +153,15 @@
     kv_part,
     q_total,
     heads,
+    cosine_ref,
+    sine_ref,
     recv_sem,
     send_sem,
     y_recv,
     y_send,
     n_recv,
     n_send,
+    load_sem,
 ):
     engine = lax.axis_index("engine")
     z = lax.axis_index("fsdp")
@@ -160,9 +174,9 @@
     groups = 4 * n_f
     tok = input_ref.shape[0]
     head = qbase_ref.shape[1]
-    piece = kvbase_ref.shape[0]
+    piece = kvbase_hbm.shape[0]
     half_groups = groups // 2
-    rank = odown_ref.shape[1]
+    mine = engine * n_f + z
     width = 2 * input_ref.shape[1]
 
     def copy(m, g, way):
@@ -226,6 +240,14 @@
 
         copy(m, g, SIB).start()
 
+    early = (n_f // 2 - 1, n_f // 2)
+
+    def relay_cross(m, g, zz):
+        if m == QUERY:
+            pl.when((zz != early[0]) & (zz != early[1]))(lambda: copy(m, g, CROSS).start())
+        else:
+            copy(m, g, CROSS).start()
+
     def along(m, d):
         @pl.when(z >= d)
         def _():
@@ -236,7 +258,7 @@
             def _():
                 copy(m, g, RIGHT).start()
 
-            copy(m, g, CROSS).start()
+            relay_cross(m, g, z - d)
             copy(m, g, SIB).start()
 
         @pl.when(z + d < n_f)
@@ -248,7 +270,7 @@
             def _():
                 copy(m, g, LEFT).start()
 
-            copy(m, g, CROSS).start()
+            relay_cross(m, g, z + d)
             copy(m, g, SIB).start()
 
     def crossing(m, d):
@@ -257,11 +279,42 @@
             copy(m, g, SIB).wait_recv()
             copy(m, g, SIB).start()
 
+        def late(zz):
+            return (zz != early[0]) & (zz != early[1]) if m == QUERY else zz >= 0
+
         if d == 0:
             take(z)
+            if m == QUERY:
+                g = across * n_f + z
+
+                @pl.when(((z == early[0]) | (z == early[1])) & (z > 0))
+                def _():
+                    copy(m, g, LEFT).start()
+
+                @pl.when(((z == early[0]) | (z == early[1])) & (z < n_f - 1))
+                def _():
+                    copy(m, g, RIGHT).start()
+
         else:
-            pl.when(z >= d)(lambda: take(z - d))
-            pl.when(z + d < n_f)(lambda: take(z + d))
+            pl.when((z >= d) & late(z - d))(lambda: take(z - d))
+            pl.when((z + d < n_f) & late(z + d))(lambda: take(z + d))
+
+    def far(m):
+        for zz in early:
+            g = across * n_f + zz
+
+            @pl.when(z != zz)
+            def _(g=g, zz=zz):
+                copy(m, g, SIB).wait_recv()
+                copy(m, g, SIB).start()
+
+                @pl.when((z < zz) & (z > 0))
+                def _():
+                    copy(m, g, LEFT).start()
+
+                @pl.when((z > zz) & (z < n_f - 1))
+                def _():
+                    copy(m, g, RIGHT).start()
 
     def from_sibling(m):
         def both(k, carry):
@@ -271,6 +324,28 @@
 
         lax.fori_loop(0, n_f, both, 0)
 
+    loads = [
+        pltpu.make_async_copy(source, target, load_sem.at[k])
+        for k, (source, target) in enumerate(
+            (
+                (kvbase_hbm, kv_buf.at[mine]),
+                (odown_hbm, odown_ref),
+                (input_hbm, input_ref),
+                (qbase_hbm, qbase_ref),
+                (qdown_hbm, qdown_ref),
+                (qup_hbm, qup_ref),
+                (gain_hbm, gain_ref),
+                (obase_hbm, obase_ref),
+                (oup_hbm, oup_ref),
+                (places_hbm, places_ref),
+                (ckeys_hbm, ckeys_ref),
+                (cvalues_hbm, cvalues_ref),
+            )
+        )
+    ]
+    for load in loads:
+        load.start()
+
     barrier = pltpu.get_barrier_semaphore()
 
     def greet(target):
@@ -282,39 +357,53 @@
     pl.when(z > 0)(lambda: greet((engine, z - 1, t)))
     pl.when(z < n_f - 1)(lambda: greet((engine, z + 1, t)))
 
-    mine = engine * n_f + z
-    kv_buf[mine] = kvbase_ref[...]
+    loads[0].wait()
+    loads[1].wait()
+    down_full[t] = odown_ref[...]
+    pl.semaphore_wait(barrier, 5 - (z == 0).astype(jnp.int32) - (z == n_f - 1).astype(jnp.int32))
+
+    own(KV)
+    to_partner(down_full, 1).start()
+    loads[2].wait()
     total = jnp.zeros((tok, 128), jnp.float32)
     for k in range(input_ref.shape[1] // 128):
         wide = input_ref[:, k * 128 : (k + 1) * 128].astype(jnp.float32)
         total = total + wide * wide
     squares[t] = total
-    down_full[t] = jnp.zeros(down_full.shape[1:], jnp.bfloat16)
-    down_full[t, :, :rank] = odown_ref[...]
-
-    pl.semaphore_wait(barrier, 5 - (z == 0).astype(jnp.int32) - (z == n_f - 1).astype(jnp.int32))
-
-    own(KV)
     to_partner(squares, 0).start()
-    to_partner(down_full, 1).start()
+
+    over_rank = (((0,), (0,)), ((), ()))
+    for k in range(3, 6):
+        loads[k].wait()
     q_buf[mine] = (
         qbase_ref[...].astype(jnp.float32)
-        + 2.0 * jnp.dot(qdown_ref[...], qup_ref[...], preferred_element_type=jnp.float32)
+        + 2.0
+        * lax.dot_general(
+            qdown_ref[...], qup_ref[...], over_rank, preferred_element_type=jnp.float32
+        )
     ).astype(jnp.bfloat16)
-
+    own(QUERY)
+
+    loads[6].wait()
     from_partner(squares, 0).wait_recv()
     mean = jnp.sum(squares[0] + squares[1], axis=1, keepdims=True) * (1.0 / width)
-    scale = lax.rsqrt(mean + 1e-05)
+    scale = jnp.broadcast_to(lax.rsqrt(mean + 1e-05), (tok, 128))
+    each = piece // 128
     for k in range(groups):
-        cut = slice(k * piece, (k + 1) * piece)
-        normed[t * groups + k] = (
-            input_ref[:, cut].astype(jnp.float32) * scale * gain_ref[:, cut].astype(jnp.float32)
-        ).astype(jnp.bfloat16)
+        for part in range(each):
+            at = k * each + part
+            normed[t * groups + k, :, part * 128 : (part + 1) * 128] = (
+                input_ref[:, at * 128 : (at + 1) * 128].astype(jnp.float32)
+                * scale
+                * gain_ref[at : at + 1, :].astype(jnp.float32)
+            ).astype(jnp.bfloat16)
         if k % 2 == 1:
             normed_copy(t, k // 2).start()
 
+    for k in range(7, len(loads)):
+        loads[k].wait()
+
     along(KV, 1)
-    own(QUERY)
     crossing(KV, 0)
     along(KV, 2)
 
@@ -324,37 +413,17 @@
         o_buf[mine, rows, :] = (
             obase_ref[rows, :].astype(jnp.float32)
             + 2.0
-            * jnp.dot(
-                down_full[side, :, :rank], oup_ref[...], preferred_element_type=jnp.float32
+            * lax.dot_general(
+                down_full[side], oup_ref[...], over_rank, preferred_element_type=jnp.float32
             )
         ).astype(jnp.bfloat16)
-
+    own(OUT)
+
+    along(QUERY, 1)
     crossing(KV, 1)
     along(KV, 3)
+    crossing(QUERY, 0)
     crossing(KV, 2)
-    along(QUERY, 1)
-    crossing(KV, 3)
-    own(OUT)
-    crossing(QUERY, 0)
-    along(QUERY, 2)
-
-    from_sibling(KV)
-    kv_part[t] = jnp.zeros(kv_part.shape[1:], jnp.float32)
-
-    def kv_step(g, carry):
-        kv_part[t] += jnp.dot(
-            normed[t * groups + g], kv_buf[g], preferred_element_type=jnp.float32
-        )
-        return carry
-
-    lax.fori_loop(0, groups // 2, kv_step, 0)
-    crossing(QUERY, 1)
-    along(QUERY, 3)
-    lax.fori_loop(groups // 2, groups, kv_step, 0)
-    to_partner(kv_part, 2).start()
-    along(OUT, 1)
-    crossing(QUERY, 2)
-    crossing(QUERY, 3)
 
     lane = lax.broadcasted_iota(jnp.int32, (tok, head), 1)
     low = lane < head // 2
@@ -362,11 +431,34 @@
     inverse = jnp.exp(index * (-2.0 / head) * jnp.log(jnp.full((tok, head), 500000.0, jnp.float32)))
     places = jnp.broadcast_to(places_ref[...].astype(jnp.float32), (head, tok)).T
     angle = places * inverse
-    cosine = jnp.cos(angle)
-    sine = jnp.where(low, -jnp.sin(angle), jnp.sin(angle))
+    cosine_ref[...] = jnp.cos(angle)
+    sine_ref[...] = jnp.where(low, -jnp.sin(angle), jnp.sin(angle))
 
     def rope(values):
-        return values * cosine + pltpu.roll(values, head // 2, 1) * sine
+        return values * cosine_ref[...] + pltpu.roll(values, head // 2, 1) * sine_ref[...]
+
+    along(QUERY, 2)
+    far(QUERY)
+    crossing(KV, 3)
+    from_sibling(KV)
+    kv_part[t] = jnp.zeros(kv_part.shape[1:], jnp.float32)
+
+    def kv_step(g, carry):
+        kv_part[t] += jnp.dot(
+            normed[t * groups + g], kv_buf[g], preferred_element_type=jnp.float32
+        )
+        return carry
+
+    lax.fori_loop(0, groups // 2, kv_step, 0)
+    along(QUERY, 3)
+    crossing(QUERY, 1)
+    along(OUT, 1)
+    lax.fori_loop(groups // 2, groups, kv_step, 0)
+    to_partner(kv_part, 2).start()
+    along(OUT, 2)
+    crossing(QUERY, 2)
+    crossing(QUERY, 3)
+    crossing(OUT, 0)
 
     from_sibling(QUERY)
     q_total[...] = jnp.zeros_like(q_total)
@@ -386,8 +478,8 @@
         return carry
 
     lax.fori_loop(0, half_groups, q_near, 0)
-    crossing(OUT, 0)
-    along(OUT, 2)
+    along(OUT, 3)
+    crossing(OUT, 1)
     lax.fori_loop(0, half_groups, q_far, 0)
 
     query = rope(q_total[...]).astype(jnp.bfloat16)
@@ -418,7 +510,6 @@
         + jnp.dot(new, new_values, preferred_element_type=jnp.float32)
     ).astype(jnp.bfloat16)
     to_partner(heads, 3).start()
-    along(OUT, 3)
     from_partner(heads, 3).wait_recv()
 
     def project(g):
@@ -436,7 +527,6 @@
 
         lax.fori_loop(0, n_f, step, 0)
 
-    crossing(OUT, 1)
     column(engine)
     crossing(OUT, 2)
     crossing(OUT, 3)
@@ -459,8 +549,22 @@
         def drain(k, carry, m=m):
             g = engine * n_f + k
             copy(m, g, SIB).wait_send()
-            copy(m, g, CROSS).wait_send()
-            copy(m, across * n_f + k, SIB).wait_send()
+            far_g = across * n_f + k
+            copy(m, far_g, SIB).wait_send()
+            first = (k == early[0]) | (k == early[1])
+            if m == QUERY:
+                pl.when(~first | (k == z))(lambda: copy(m, g, CROSS).wait_send())
+
+                @pl.when(first & (z > 0) & (k >= z))
+                def _():
+                    copy(m, far_g, LEFT).wait_send()
+
+                @pl.when(first & (z < n_f - 1) & (k <= z))
+                def _():
+                    copy(m, far_g, RIGHT).wait_send()
+
+            else:
+                copy(m, g, CROSS).wait_send()
 
             @pl.when((z > 0) & (k >= z))
             def _():
@@ -503,48 +607,64 @@
 ):
     tok, features = layer_input.shape
     depth, head = query_base.shape
+    rank = query_up.shape[0]
     groups = 4 * n_f
     kv_base = kv_base[0]
     output_base_weight = output_base_weight[:, 0]
     output_up_factor = output_up_factor[:, 0]
     piece = kv_base.shape[0]
     vmem = pl.BlockSpec(memory_space=pltpu.VMEM)
+    hbm = pl.BlockSpec(memory_space=pltpu.HBM)
     smem = pl.BlockSpec(memory_space=pltpu.SMEM)
     dma = pltpu.SemaphoreType.DMA
     return pl.pallas_call(
         functools.partial(kernel, n_f),
         out_shape=jax.ShapeDtypeStruct((tok, features), jnp.bfloat16),
-        in_specs=[vmem] * 12 + [smem],
+        in_specs=[hbm] * 12 + [smem],
         out_specs=vmem,
         scratch_shapes=[
+            pltpu.VMEM((tok, features), jnp.bfloat16),
+            pltpu.VMEM((features // 128, 128), jnp.bfloat16),
+            pltpu.VMEM(query_base.shape, jnp.bfloat16),
+            pltpu.VMEM((rank, depth), jnp.bfloat16),
+            pltpu.VMEM(query_up.shape, jnp.bfloat16),
+            pltpu.VMEM(output_base_weight.shape, jnp.bfloat16),
+            pltpu.VMEM((rank, head), jnp.bfloat16),
+            pltpu.VMEM(output_up_factor.shape, jnp.bfloat16),
+            pltpu.VMEM(cache_keys.shape[1:], jnp.bfloat16),
+            pltpu.VMEM(cache_values.shape[1:], jnp.bfloat16),
+            pltpu.VMEM(positions.shape, jnp.int32),
             pltpu.VMEM((groups,) + kv_base.shape, jnp.bfloat16),
             pltpu.VMEM((groups,) + query_base.shape, jnp.bfloat16),
             pltpu.VMEM((groups,) + output_base_weight.shape, jnp.bfloat16),
             pltpu.VMEM((2 * groups, tok, piece), jnp.bfloat16),
             pltpu.VMEM((2, tok, 128), jnp.float32),
-            pltpu.VMEM((2, head, 128), jnp.bfloat16),
+            pltpu.VMEM((2, rank, head), jnp.bfloat16),
             pltpu.VMEM((2, tok, 2 * head), jnp.float32),
             pltpu.VMEM((tok, head), jnp.float32),
             pltpu.VMEM((2, tok, head), jnp.bfloat16),
+            pltpu.VMEM((tok, head), jnp.float32),
+            pltpu.VMEM((tok, head), jnp.float32),
             dma((3, groups)),
             dma((3, 4, groups)),
             dma((4,)),
             dma((4,)),
             dma((groups // 2,)),
             dma((groups // 2,)),
+            dma((12,)),
         ],
         compiler_params=pltpu.CompilerParams(
             collective_id=0, has_side_effects=True, vmem_limit_bytes=48 * 1024 * 1024
         ),
     )(
         layer_input,
-        norm_gain[None, :],
+        norm_gain.reshape(-1, 128),
         query_base,
-        query_down,
+        query_down.T,
         query_up,
         kv_base,
         output_base_weight,
-        output_down_factor,
+        output_down_factor.T,
         output_up_factor,
         cache_keys[0],
         cache_values[0],

time: 96 us -> 105 us (1.094)
  Pallas kernels: 81.8 us -> 91.5 us
    pallas_call x1, Pallas kernels: 81.8 us -> 91.5 us  [per_device(): pl.pallas_call(functools.partial(kernel, n_f), out_shape=jax.ShapeDtypeSt...]
    unnamed x21 -> x25, local copies, waits for them, and re-layouts: 11.7 us -> 12.1 us
where the time goes in v2:
time: 105 us; the launch traced here: 104 us
  Pallas kernels  91.5 us (87%)
  local copies, waits for them, and re-layouts  12.1 us (12%)
    pallas_call x1, Pallas kernels, per_device(): pl.pallas_call(functools.partial(kernel, n_f), out_shape=jax.ShapeDtypeSt...  91.5 us
    unnamed x25, local copies, waits for them, and re-layouts  12.1 us

profile of v2, /device:TPU:1, one launch (start us, length us, event | category | flops | bytes accessed | tf_op | source)
XLA Modules:
  0.0 104.3 jit_solution(15223527018260529294)
XLA Ops:
  0.7 0.0 copy-start
  0.7 1.6 %copy-done = bf16[128,8192]{1,0:T(8,128)(2,1)S(1)} copy-done((bf16[128,8192]{1,0:T(8,128)(2,1)S(1)}, bf16[128,8192]{1,0:T(8,128)(2,1)}, u32[]{:S(2)}) %copy-start) | copy-done | bytes 2097176
  2.2 0.0 copy-start.1
  2.2 0.9 copy-done.1
  3.2 0.0 copy-start.2
  3.2 0.9 copy-done.2
  4.1 0.0 copy-start.3
  4.1 0.9 copy-done.3
  5.1 0.0 copy-start.4
  5.1 0.9 copy-done.4
  6.0 0.0 copy-start.5
  6.0 0.9 copy-done.5
  6.9 0.0 copy-start.6
  6.9 0.9 copy-done.6
  7.8 0.0 copy-start.7
  7.8 0.8 copy-done.7
  8.7 0.0 copy-start.8
  8.7 0.7 copy-done.8
  9.4 0.7 copy-done.9
  10.1 0.0 copy-start.10
  10.1 0.7 copy-done.10
  10.8 0.7 copy-done.11
  11.5 91.5 %shard_map.127 = bf16[128,8192]{1,0:T(8,128)(2,1)S(1)} custom-call(bf16[128,8192]{1,0:T(8,128)(2,1)S(1)} %copy-done, bf16[64,128]{1,0:T(8,128)(2,1)S(1)} %bitcast.14, bf16[1024,128]{1,0:T(8,128)(2,1)S(1)} %copy-done.1, bf16[64,1024]{1,0:T(8,128)(2,1)S(1)} %bitcast.10, bf16[64,128]{1,0:T(8,128)(2,1)S(1)} %copy-done.9, bf16[512,256]{1,0:T(8,128)(2,1)S(1)} %bitcast.8, ...), custom_call_target="tpu_custom_call" | custom-call | tf_op jit(solution)/shard_map/pallas_call | solution.py:620
  103.0 1.3 %copy.16 = bf16[128,8192]{1,0:T(8,128)(2,1)} copy(bf16[128,8192]{1,0:T(8,128)(2,1)S(1)} %shard_map.127) | data formatting | bytes 4194304
  (2 shorter events, 0.0 us)
Async XLA Ops:
  0.7 1.6 %copy-start = (bf16[128,8192]{1,0:T(8,128)(2,1)S(1)}, bf16[128,8192]{1,0:T(8,128)(2,1)}, u32[]{:S(2)}) copy-start(bf16[128,8192]{1,0:T(8,128)(2,1)} %input_hbm.1) | copy-start | bytes 6291460
  2.2 0.9 copy-start.1
  3.2 0.9 copy-start.2
  4.1 0.9 copy-start.3
  5.1 0.9 copy-start.4
  6.0 0.9 copy-start.5
  6.9 0.9 copy-start.6
  7.8 0.8 copy-start.7
  8.7 0.7 copy-start.8
  9.4 0.7 copy-start.9
  10.1 0.7 copy-start.10
  10.8 0.7 copy-start.11

commit v3 on v2

--- a/solution.py
+++ b/solution.py
@@ -243,7 +243,7 @@
     early = (n_f // 2 - 1, n_f // 2)
 
     def relay_cross(m, g, zz):
-        if m == QUERY:
+        if m == KV:
             pl.when((zz != early[0]) & (zz != early[1]))(lambda: copy(m, g, CROSS).start())
         else:
             copy(m, g, CROSS).start()
@@ -280,11 +280,11 @@
             copy(m, g, SIB).start()
 
         def late(zz):
-            return (zz != early[0]) & (zz != early[1]) if m == QUERY else zz >= 0
+            return (zz != early[0]) & (zz != early[1]) if m == KV else zz >= 0
 
         if d == 0:
             take(z)
-            if m == QUERY:
+            if m == KV:
                 g = across * n_f + z
 
                 @pl.when(((z == early[0]) | (z == early[1])) & (z > 0))
@@ -300,7 +300,8 @@
             pl.when((z + d < n_f) & late(z + d))(lambda: take(z + d))
 
     def far(m):
-        for zz in early:
+        for k in range(2):
+            zz = jnp.where(z < n_f // 2, early[k], early[1 - k])
             g = across * n_f + zz
 
             @pl.when(z != zz)
@@ -403,8 +404,8 @@
     for k in range(7, len(loads)):
         loads[k].wait()
 
+    crossing(KV, 0)
     along(KV, 1)
-    crossing(KV, 0)
     along(KV, 2)
 
     from_partner(down_full, 1).wait_recv()
@@ -419,11 +420,9 @@
         ).astype(jnp.bfloat16)
     own(OUT)
 
+    far(KV)
     along(QUERY, 1)
-    crossing(KV, 1)
     along(KV, 3)
-    crossing(QUERY, 0)
-    crossing(KV, 2)
 
     lane = lax.broadcasted_iota(jnp.int32, (tok, head), 1)
     low = lane < head // 2
@@ -438,8 +437,12 @@
         return values * cosine_ref[...] + pltpu.roll(values, head // 2, 1) * sine_ref[...]
 
     along(QUERY, 2)
-    far(QUERY)
+    along(QUERY, 3)
+    crossing(KV, 1)
+    crossing(KV, 2)
     crossing(KV, 3)
+    along(OUT, 1)
+    crossing(QUERY, 0)
     from_sibling(KV)
     kv_part[t] = jnp.zeros(kv_part.shape[1:], jnp.float32)
 
@@ -450,12 +453,11 @@
         return carry
 
     lax.fori_loop(0, groups // 2, kv_step, 0)
-    along(QUERY, 3)
-    crossing(QUERY, 1)
-    along(OUT, 1)
+    along(OUT, 2)
     lax.fori_loop(groups // 2, groups, kv_step, 0)
     to_partner(kv_part, 2).start()
-    along(OUT, 2)
+    along(OUT, 3)
+    crossing(QUERY, 1)
     crossing(QUERY, 2)
     crossing(QUERY, 3)
     crossing(OUT, 0)
@@ -478,7 +480,6 @@
         return carry
 
     lax.fori_loop(0, half_groups, q_near, 0)
-    along(OUT, 3)
     crossing(OUT, 1)
     lax.fori_loop(0, half_groups, q_far, 0)
 
@@ -552,7 +553,7 @@
             far_g = across * n_f + k
             copy(m, far_g, SIB).wait_send()
             first = (k == early[0]) | (k == early[1])
-            if m == QUERY:
+            if m == KV:
                 pl.when(~first | (k == z))(lambda: copy(m, g, CROSS).wait_send())
 
                 @pl.when(first & (z > 0) & (k >= z))
@@ -654,7 +655,7 @@
             dma((12,)),
         ],
         compiler_params=pltpu.CompilerParams(
-            collective_id=0, has_side_effects=True, vmem_limit_bytes=48 * 1024 * 1024
+            collective_id=0, has_side_effects=True, vmem_limit_bytes=60 * 1024 * 1024
         ),
     )(
         layer_input,

time: 105 us -> 96.5 us (0.919)
  local copies, waits for them, and re-layouts: 12.1 us -> 3.1 us
    unnamed x25 -> x1, local copies, waits for them, and re-layouts: 12.1 us -> 3.1 us
where the time goes in v3:
time: 96.5 us; the launch traced here: 95.2 us
  Pallas kernels  91.4 us (95%)
  local copies, waits for them, and re-layouts  3.1 us (3%)
    pallas_call x1, Pallas kernels, per_device(): pl.pallas_call(functools.partial(kernel, n_f), out_shape=jax.ShapeDtypeSt...  91.4 us
    unnamed x1, local copies, waits for them, and re-layouts  3.1 us

profile of v3, /device:TPU:1, one launch (start us, length us, event | category | flops | bytes accessed | tf_op | source)
XLA Modules:
  0.0 95.2 jit_solution(5868692831753215071)
XLA Ops:
  0.7 91.4 %shard_map.127 = bf16[128,8192]{1,0:T(8,128)(2,1)} custom-call(bf16[128,8192]{1,0:T(8,128)(2,1)} %input_hbm.1, bf16[64,128]{1,0:T(8,128)(2,1)} %bitcast.14, bf16[1024,128]{1,0:T(8,128)(2,1)} %qbase_hbm.1, bf16[64,1024]{1,0:T(8,128)(2,1)} %bitcast.10, bf16[64,128]{1,0:T(8,128)(2,1)} %qup_hbm.1, bf16[512,256]{1,0:T(8,128)(2,1)} %bitcast.8, ...), custom_call_target="tpu_custom_call" | custom-call | tf_op jit(solution)/shard_map/pallas_call | solution.py:621
  92.1 3.1 %copy.16 = bf16[128,8192]{1,0:T(8,128)(2,1)} copy(bf16[128,8192]{1,0:T(8,128)(2,1)} %shard_map.127) | data formatting | bytes 4194304

commit v4 on v3

--- a/solution.py
+++ b/solution.py
@@ -153,6 +153,7 @@
     kv_part,
     q_total,
     heads,
+    both,
     cosine_ref,
     sine_ref,
     recv_sem,
@@ -240,14 +241,6 @@
 
         copy(m, g, SIB).start()
 
-    early = (n_f // 2 - 1, n_f // 2)
-
-    def relay_cross(m, g, zz):
-        if m == KV:
-            pl.when((zz != early[0]) & (zz != early[1]))(lambda: copy(m, g, CROSS).start())
-        else:
-            copy(m, g, CROSS).start()
-
     def along(m, d):
         @pl.when(z >= d)
         def _():
@@ -258,7 +251,7 @@
             def _():
                 copy(m, g, RIGHT).start()
 
-            relay_cross(m, g, z - d)
+            copy(m, g, CROSS).start()
             copy(m, g, SIB).start()
 
         @pl.when(z + d < n_f)
@@ -270,7 +263,7 @@
             def _():
                 copy(m, g, LEFT).start()
 
-            relay_cross(m, g, z + d)
+            copy(m, g, CROSS).start()
             copy(m, g, SIB).start()
 
     def crossing(m, d):
@@ -279,51 +272,19 @@
             copy(m, g, SIB).wait_recv()
             copy(m, g, SIB).start()
 
-        def late(zz):
-            return (zz != early[0]) & (zz != early[1]) if m == KV else zz >= 0
-
         if d == 0:
             take(z)
-            if m == KV:
-                g = across * n_f + z
-
-                @pl.when(((z == early[0]) | (z == early[1])) & (z > 0))
-                def _():
-                    copy(m, g, LEFT).start()
-
-                @pl.when(((z == early[0]) | (z == early[1])) & (z < n_f - 1))
-                def _():
-                    copy(m, g, RIGHT).start()
-
         else:
-            pl.when((z >= d) & late(z - d))(lambda: take(z - d))
-            pl.when((z + d < n_f) & late(z + d))(lambda: take(z + d))
-
-    def far(m):
-        for k in range(2):
-            zz = jnp.where(z < n_f // 2, early[k], early[1 - k])
-            g = across * n_f + zz
-
-            @pl.when(z != zz)
-            def _(g=g, zz=zz):
-                copy(m, g, SIB).wait_recv()
-                copy(m, g, SIB).start()
-
-                @pl.when((z < zz) & (z > 0))
-                def _():
-                    copy(m, g, LEFT).start()
-
-                @pl.when((z > zz) & (z < n_f - 1))
-                def _():
-                    copy(m, g, RIGHT).start()
+            pl.when(z >= d)(lambda: take(z - d))
+            pl.when(z + d < n_f)(lambda: take(z + d))
 
     def from_sibling(m):
-        def both(k, carry):
+        def arrived(k, carry):
             copy(m, sibling * n_f + k, SIB).wait_recv()
             copy(m, lax.rem(sibling + 2, 4) * n_f + k, SIB).wait_recv()
             return carry
 
-        lax.fori_loop(0, n_f, both, 0)
+        lax.fori_loop(0, n_f, arrived, 0)
 
     loads = [
         pltpu.make_async_copy(source, target, load_sem.at[k])
@@ -404,7 +365,6 @@
     for k in range(7, len(loads)):
         loads[k].wait()
 
-    crossing(KV, 0)
     along(KV, 1)
     along(KV, 2)
 
@@ -420,9 +380,9 @@
         ).astype(jnp.bfloat16)
     own(OUT)
 
-    far(KV)
     along(QUERY, 1)
     along(KV, 3)
+    crossing(KV, 0)
 
     lane = lax.broadcasted_iota(jnp.int32, (tok, head), 1)
     low = lane < head // 2
@@ -437,12 +397,13 @@
         return values * cosine_ref[...] + pltpu.roll(values, head // 2, 1) * sine_ref[...]
 
     along(QUERY, 2)
+    crossing(KV, 1)
     along(QUERY, 3)
-    crossing(KV, 1)
     crossing(KV, 2)
+    along(OUT, 1)
     crossing(KV, 3)
-    along(OUT, 1)
     crossing(QUERY, 0)
+    along(OUT, 2)
     from_sibling(KV)
     kv_part[t] = jnp.zeros(kv_part.shape[1:], jnp.float32)
 
@@ -453,11 +414,10 @@
         return carry
 
     lax.fori_loop(0, groups // 2, kv_step, 0)
-    along(OUT, 2)
+    crossing(QUERY, 1)
+    along(OUT, 3)
     lax.fori_loop(groups // 2, groups, kv_step, 0)
     to_partner(kv_part, 2).start()
-    along(OUT, 3)
-    crossing(QUERY, 1)
     crossing(QUERY, 2)
     crossing(QUERY, 3)
     crossing(OUT, 0)
@@ -506,66 +466,57 @@
     summed = jnp.sum(old, axis=1, keepdims=True) + jnp.sum(new, axis=1, keepdims=True)
     old = (old / summed).astype(jnp.bfloat16)
     new = (new / summed).astype(jnp.bfloat16)
-    heads[t] = (
+    own_head = (
         jnp.dot(old, cvalues_ref[...], preferred_element_type=jnp.float32)
         + jnp.dot(new, new_values, preferred_element_type=jnp.float32)
     ).astype(jnp.bfloat16)
+    heads[t] = own_head
     to_partner(heads, 3).start()
     from_partner(heads, 3).wait_recv()
 
+    both[:, :head] = heads[0]
+    both[:, head:] = heads[1]
+
     def project(g):
-        first = jnp.dot(heads[0], o_buf[g, :head, :], preferred_element_type=jnp.float32)
-        second = jnp.dot(heads[1], o_buf[g, head:, :], preferred_element_type=jnp.float32)
-        both = first.astype(jnp.bfloat16).astype(jnp.float32) + second.astype(
-            jnp.bfloat16
-        ).astype(jnp.float32)
-        result_ref[:, pl.ds(pl.multiple_of(g * piece, piece), piece)] = both.astype(jnp.bfloat16)
-
-    def column(which):
-        def step(k, carry):
-            project(which * n_f + k)
-            return carry
-
-        lax.fori_loop(0, n_f, step, 0)
-
-    column(engine)
-    crossing(OUT, 2)
-    crossing(OUT, 3)
-    column(across)
-
-    def sibling_column(which):
-        def step(k, carry):
-            g = which * n_f + k
+        result_ref[:, pl.ds(pl.multiple_of(g * piece, piece), piece)] = jnp.dot(
+            both[...], o_buf[g], preferred_element_type=jnp.float32
+        ).astype(jnp.bfloat16)
+
+    def near(k, carry):
+        project(engine * n_f + k)
+        g = sibling * n_f + k
+        copy(OUT, g, SIB).wait_recv()
+        project(g)
+        return carry
+
+    def crossed(d):
+        def pair(zz):
+            project(across * n_f + zz)
+            g = lax.rem(sibling + 2, 4) * n_f + zz
             copy(OUT, g, SIB).wait_recv()
             project(g)
-            return carry
-
-        lax.fori_loop(0, n_f, step, 0)
-
-    sibling_column(sibling)
-    sibling_column(lax.rem(sibling + 2, 4))
+
+        if d == 0:
+            pair(z)
+        else:
+            pl.when(z >= d)(lambda: pair(z - d))
+            pl.when(z + d < n_f)(lambda: pair(z + d))
+
+    lax.fori_loop(0, n_f, near, 0)
+    crossing(OUT, 2)
+    crossed(0)
+    crossed(1)
+    crossing(OUT, 3)
+    crossed(2)
+    crossed(3)
 
     for m in range(3):
 
         def drain(k, carry, m=m):
             g = engine * n_f + k
             copy(m, g, SIB).wait_send()
-            far_g = across * n_f + k
-            copy(m, far_g, SIB).wait_send()
-            first = (k == early[0]) | (k == early[1])
-            if m == KV:
-                pl.when(~first | (k == z))(lambda: copy(m, g, CROSS).wait_send())
-
-                @pl.when(first & (z > 0) & (k >= z))
-                def _():
-                    copy(m, far_g, LEFT).wait_send()
-
-                @pl.when(first & (z < n_f - 1) & (k <= z))
-                def _():
-                    copy(m, far_g, RIGHT).wait_send()
-
-            else:
-                copy(m, g, CROSS).wait_send()
+            copy(m, g, CROSS).wait_send()
+            copy(m, across * n_f + k, SIB).wait_send()
 
             @pl.when((z > 0) & (k >= z))
             def _():
@@ -644,6 +595,7 @@
             pltpu.VMEM((2, tok, 2 * head), jnp.float32),
             pltpu.VMEM((tok, head), jnp.float32),
             pltpu.VMEM((2, tok, head), jnp.bfloat16),
+            pltpu.VMEM((tok, 2 * head), jnp.bfloat16),
             pltpu.VMEM((tok, head), jnp.float32),
             pltpu.VMEM((tok, head), jnp.float32),
             dma((3, groups)),

time: 96.5 us -> 83.9 us (0.87)
  Pallas kernels: 91.4 us -> 79.2 us
    pallas_call x1, Pallas kernels: 91.4 us -> 79.2 us  [per_device(): pl.pallas_call(functools.partial(kernel, n_f), out_shape=jax.ShapeDtypeSt...]
where the time goes in v4:
time: 83.9 us; the launch traced here: 83 us
  Pallas kernels  79.2 us (94%)
  local copies, waits for them, and re-layouts  3.1 us (4%)
    pallas_call x1, Pallas kernels, per_device(): pl.pallas_call(functools.partial(kernel, n_f), out_shape=jax.ShapeDtypeSt...  79.2 us
    unnamed x1, local copies, waits for them, and re-layouts  3.1 us

profile of v4, /device:TPU:1, one launch (start us, length us, event | category | flops | bytes accessed | tf_op | source)
XLA Modules:
  0.0 83.0 jit_solution(7487503684335896062)
XLA Ops:
  0.7 79.2 %shard_map.127 = bf16[128,8192]{1,0:T(8,128)(2,1)} custom-call(bf16[128,8192]{1,0:T(8,128)(2,1)} %input_hbm.1, bf16[64,128]{1,0:T(8,128)(2,1)} %bitcast.14, bf16[1024,128]{1,0:T(8,128)(2,1)} %qbase_hbm.1, bf16[64,1024]{1,0:T(8,128)(2,1)} %bitcast.10, bf16[64,128]{1,0:T(8,128)(2,1)} %qup_hbm.1, bf16[512,256]{1,0:T(8,128)(2,1)} %bitcast.8, ...), custom_call_target="tpu_custom_call" | custom-call | tf_op jit(solution)/shard_map/pallas_call | solution.py:572
  79.9 3.1 %copy.16 = bf16[128,8192]{1,0:T(8,128)(2,1)} copy(bf16[128,8192]{1,0:T(8,128)(2,1)} %shard_map.127) | data formatting | bytes 4194304

commit v5 on v4

--- a/solution.py
+++ b/solution.py
@@ -241,6 +241,17 @@
 
         copy(m, g, SIB).start()
 
+    last = n_f - 1
+
+    def at_end(zz):
+        return (zz == 0) | (zz == last)
+
+    def relay_cross(m, g, zz):
+        if m == KV:
+            pl.when((zz > 0) & (zz < last))(lambda: copy(m, g, CROSS).start())
+        else:
+            copy(m, g, CROSS).start()
+
     def along(m, d):
         @pl.when(z >= d)
         def _():
@@ -251,7 +262,7 @@
             def _():
                 copy(m, g, RIGHT).start()
 
-            copy(m, g, CROSS).start()
+            relay_cross(m, g, z - d)
             copy(m, g, SIB).start()
 
         @pl.when(z + d < n_f)
@@ -263,7 +274,22 @@
             def _():
                 copy(m, g, LEFT).start()
 
-            copy(m, g, CROSS).start()
+            relay_cross(m, g, z + d)
+            copy(m, g, SIB).start()
+
+    def far(m):
+        @pl.when(z > 0)
+        def _():
+            g = across * n_f
+            copy(m, g, SIB).wait_recv()
+            pl.when(z < last)(lambda: copy(m, g, RIGHT).start())
+            copy(m, g, SIB).start()
+
+        @pl.when(z < last)
+        def _():
+            g = across * n_f + last
+            copy(m, g, SIB).wait_recv()
+            pl.when(z > 0)(lambda: copy(m, g, LEFT).start())
             copy(m, g, SIB).start()
 
     def crossing(m, d):
@@ -272,11 +298,18 @@
             copy(m, g, SIB).wait_recv()
             copy(m, g, SIB).start()
 
+        def late(zz):
+            return (zz > 0) & (zz < last) if m == KV else zz >= 0
+
         if d == 0:
             take(z)
+            if m == KV:
+                g = across * n_f + z
+                pl.when(z == 0)(lambda: copy(m, g, RIGHT).start())
+                pl.when(z == last)(lambda: copy(m, g, LEFT).start())
         else:
-            pl.when(z >= d)(lambda: take(z - d))
-            pl.when(z + d < n_f)(lambda: take(z + d))
+            pl.when((z >= d) & late(z - d))(lambda: take(z - d))
+            pl.when((z + d < n_f) & late(z + d))(lambda: take(z + d))
 
     def from_sibling(m):
         def arrived(k, carry):
@@ -366,7 +399,9 @@
         loads[k].wait()
 
     along(KV, 1)
+    crossing(KV, 0)
     along(KV, 2)
+    far(KV)
 
     from_partner(down_full, 1).wait_recv()
     for side in range(2):
@@ -378,11 +413,8 @@
                 down_full[side], oup_ref[...], over_rank, preferred_element_type=jnp.float32
             )
         ).astype(jnp.bfloat16)
-    own(OUT)
-
     along(QUERY, 1)
     along(KV, 3)
-    crossing(KV, 0)
 
     lane = lax.broadcasted_iota(jnp.int32, (tok, head), 1)
     low = lane < head // 2
@@ -397,6 +429,7 @@
         return values * cosine_ref[...] + pltpu.roll(values, head // 2, 1) * sine_ref[...]
 
     along(QUERY, 2)
+    own(OUT)
     crossing(KV, 1)
     along(QUERY, 3)
     crossing(KV, 2)
@@ -515,8 +548,14 @@
         def drain(k, carry, m=m):
             g = engine * n_f + k
             copy(m, g, SIB).wait_send()
-            copy(m, g, CROSS).wait_send()
-            copy(m, across * n_f + k, SIB).wait_send()
+            far_g = across * n_f + k
+            copy(m, far_g, SIB).wait_send()
+            if m == KV:
+                pl.when(~at_end(k) | (k == z))(lambda: copy(m, g, CROSS).wait_send())
+                pl.when((k == 0) & (z < last))(lambda: copy(m, far_g, RIGHT).wait_send())
+                pl.when((k == last) & (z > 0))(lambda: copy(m, far_g, LEFT).wait_send())
+            else:
+                copy(m, g, CROSS).wait_send()
 
             @pl.when((z > 0) & (k >= z))
             def _():

time: 83.9 us -> 91.3 us (1.088)
  Pallas kernels: 79.2 us -> 87.4 us
    pallas_call x1, Pallas kernels: 79.2 us -> 87.4 us  [per_device(): pl.pallas_call(functools.partial(kernel, n_f), out_shape=jax.ShapeDtypeSt...]
where the time goes in v5:
time: 91.3 us; the launch traced here: 91.2 us
  Pallas kernels  87.4 us (96%)
  local copies, waits for them, and re-layouts  3.1 us (3%)
    pallas_call x1, Pallas kernels, per_device(): pl.pallas_call(functools.partial(kernel, n_f), out_shape=jax.ShapeDtypeSt...  87.4 us
    unnamed x1, local copies, waits for them, and re-layouts  3.1 us

profile of v5, /device:TPU:1, one launch (start us, length us, event | category | flops | bytes accessed | tf_op | source)
XLA Modules:
  0.0 91.2 jit_solution(12115142782971985966)
XLA Ops:
  0.7 87.4 %shard_map.127 = bf16[128,8192]{1,0:T(8,128)(2,1)} custom-call(bf16[128,8192]{1,0:T(8,128)(2,1)} %input_hbm.1, bf16[64,128]{1,0:T(8,128)(2,1)} %bitcast.14, bf16[1024,128]{1,0:T(8,128)(2,1)} %qbase_hbm.1, bf16[64,1024]{1,0:T(8,128)(2,1)} %bitcast.10, bf16[64,128]{1,0:T(8,128)(2,1)} %qup_hbm.1, bf16[512,256]{1,0:T(8,128)(2,1)} %bitcast.8, ...), custom_call_target="tpu_custom_call" | custom-call | tf_op jit(solution)/shard_map/pallas_call | solution.py:611
  88.1 3.1 %copy.16 = bf16[128,8192]{1,0:T(8,128)(2,1)} copy(bf16[128,8192]{1,0:T(8,128)(2,1)} %shard_map.127) | data formatting | bytes 4194304

commit v6 on v4

--- a/solution.py
+++ b/solution.py
@@ -418,30 +418,55 @@
     along(OUT, 3)
     lax.fori_loop(groups // 2, groups, kv_step, 0)
     to_partner(kv_part, 2).start()
-    crossing(QUERY, 2)
-    crossing(QUERY, 3)
-    crossing(OUT, 0)
-
-    from_sibling(QUERY)
+
     q_total[...] = jnp.zeros_like(q_total)
+    local = engine // 2 == t
 
     def q_step(g):
+        @pl.when(g // half_groups != t)
+        def _():
+            normed_copy(other, lax.rem(g, half_groups)).wait_recv()
+
         q_total[...] += jnp.dot(
             normed[2 * g], q_buf[g, :piece, :], preferred_element_type=jnp.float32
         ) + jnp.dot(normed[2 * g + 1], q_buf[g, piece:, :], preferred_element_type=jnp.float32)
 
-    def q_near(k, carry):
-        q_step(t * half_groups + k)
-        return carry
-
-    def q_far(k, carry):
-        normed_copy(other, k).wait_recv()
-        q_step(other * half_groups + k)
-        return carry
-
-    lax.fori_loop(0, half_groups, q_near, 0)
-    crossing(OUT, 1)
-    lax.fori_loop(0, half_groups, q_far, 0)
+    def q_column():
+        def step(k, carry):
+            q_step(engine * n_f + k)
+            g = sibling * n_f + k
+            copy(QUERY, g, SIB).wait_recv()
+            q_step(g)
+            return carry
+
+        lax.fori_loop(0, n_f, step, 0)
+
+    def q_crossed(d):
+        def pair(zz):
+            q_step(across * n_f + zz)
+            g = lax.rem(sibling + 2, 4) * n_f + zz
+            copy(QUERY, g, SIB).wait_recv()
+            q_step(g)
+
+        if d == 0:
+            pair(z)
+        else:
+            pl.when(z >= d)(lambda: pair(z - d))
+            pl.when(z + d < n_f)(lambda: pair(z + d))
+
+    def q_first():
+        q_crossed(0)
+        q_crossed(1)
+
+    pl.when(local)(q_column)
+    pl.when(jnp.logical_not(local))(q_first)
+    crossing(QUERY, 2)
+    pl.when(local)(q_first)
+    pl.when(jnp.logical_not(local))(q_column)
+    crossing(QUERY, 3)
+    crossing(OUT, 0)
+    q_crossed(2)
+    q_crossed(3)
 
     query = rope(q_total[...]).astype(jnp.bfloat16)
     from_partner(kv_part, 2).wait_recv()
@@ -472,6 +497,7 @@
     ).astype(jnp.bfloat16)
     heads[t] = own_head
     to_partner(heads, 3).start()
+    crossing(OUT, 1)
     from_partner(heads, 3).wait_recv()
 
     both[:, :head] = heads[0]

time: 83.9 us -> 83.1 us (level)
  no operation moved by 1% of the time
where the time goes in v6:
time: 83.1 us; the launch traced here: 83 us
  Pallas kernels  79.2 us (95%)
  local copies, waits for them, and re-layouts  3.1 us (4%)
    pallas_call x1, Pallas kernels, per_device(): pl.pallas_call(functools.partial(kernel, n_f), out_shape=jax.ShapeDtypeSt...  79.2 us
    unnamed x1, local copies, waits for them, and re-layouts  3.1 us

profile of v6, /device:TPU:1, one launch (start us, length us, event | category | flops | bytes accessed | tf_op | source)
XLA Modules:
  0.0 83.0 jit_solution(13567012996326721941)
XLA Ops:
  0.7 79.2 %shard_map.127 = bf16[128,8192]{1,0:T(8,128)(2,1)} custom-call(bf16[128,8192]{1,0:T(8,128)(2,1)} %input_hbm.1, bf16[64,128]{1,0:T(8,128)(2,1)} %bitcast.14, bf16[1024,128]{1,0:T(8,128)(2,1)} %qbase_hbm.1, bf16[64,1024]{1,0:T(8,128)(2,1)} %bitcast.10, bf16[64,128]{1,0:T(8,128)(2,1)} %qup_hbm.1, bf16[512,256]{1,0:T(8,128)(2,1)} %bitcast.8, ...), custom_call_target="tpu_custom_call" | custom-call | tf_op jit(solution)/shard_map/pallas_call | solution.py:598
  79.9 3.1 %copy.16 = bf16[128,8192]{1,0:T(8,128)(2,1)} copy(bf16[128,8192]{1,0:T(8,128)(2,1)} %shard_map.127) | data formatting | bytes 4194304

commit v7 on v6

--- a/solution.py
+++ b/solution.py
@@ -163,6 +163,8 @@
     n_recv,
     n_send,
     load_sem,
+    out_buf,
+    out_sem,
 ):
     engine = lax.axis_index("engine")
     z = lax.axis_index("fsdp")
@@ -503,10 +505,18 @@
     both[:, :head] = heads[0]
     both[:, head:] = heads[1]
 
+    def written(g):
+        return pltpu.make_async_copy(
+            out_buf.at[g],
+            result_ref.at[:, pl.ds(pl.multiple_of(g * piece, piece), piece)],
+            out_sem.at[g],
+        )
+
     def project(g):
-        result_ref[:, pl.ds(pl.multiple_of(g * piece, piece), piece)] = jnp.dot(
+        out_buf[g] = jnp.dot(
             both[...], o_buf[g], preferred_element_type=jnp.float32
         ).astype(jnp.bfloat16)
+        written(g).start()
 
     def near(k, carry):
         project(engine * n_f + k)
@@ -561,6 +571,12 @@
         return carry
 
     lax.fori_loop(0, half_groups, drain_normed, 0)
+
+    def drain_out(g, carry):
+        written(g).wait()
+        return carry
+
+    lax.fori_loop(0, groups, drain_out, 0)
     to_partner(squares, 0).wait_send()
     to_partner(down_full, 1).wait_send()
     to_partner(kv_part, 2).wait_send()
@@ -591,7 +607,6 @@
     output_base_weight = output_base_weight[:, 0]
     output_up_factor = output_up_factor[:, 0]
     piece = kv_base.shape[0]
-    vmem = pl.BlockSpec(memory_space=pltpu.VMEM)
     hbm = pl.BlockSpec(memory_space=pltpu.HBM)
     smem = pl.BlockSpec(memory_space=pltpu.SMEM)
     dma = pltpu.SemaphoreType.DMA
@@ -599,7 +614,7 @@
         functools.partial(kernel, n_f),
         out_shape=jax.ShapeDtypeStruct((tok, features), jnp.bfloat16),
         in_specs=[hbm] * 12 + [smem],
-        out_specs=vmem,
+        out_specs=hbm,
         scratch_shapes=[
             pltpu.VMEM((tok, features), jnp.bfloat16),
             pltpu.VMEM((features // 128, 128), jnp.bfloat16),
@@ -631,6 +646,8 @@
             dma((groups // 2,)),
             dma((groups // 2,)),
             dma((12,)),
+            pltpu.VMEM((groups, tok, piece), jnp.bfloat16),
+            dma((groups,)),
         ],
         compiler_params=pltpu.CompilerParams(
             collective_id=0, has_side_effects=True, vmem_limit_bytes=60 * 1024 * 1024

time: 83.1 us -> 82.3 us (level)
  no operation moved by 1% of the time
where the time goes in v7:
time: 82.3 us; the launch traced here: 82.1 us
  Pallas kernels  78.4 us (95%)
  local copies, waits for them, and re-layouts  3.1 us (4%)
    pallas_call x1, Pallas kernels, per_device(): pl.pallas_call(functools.partial(kernel, n_f), out_shape=jax.ShapeDtypeSt...  78.4 us
    unnamed x1, local copies, waits for them, and re-layouts  3.1 us

profile of v7, /device:TPU:1, one launch (start us, length us, event | category | flops | bytes accessed | tf_op | source)
XLA Modules:
  0.0 82.1 jit_solution(2692026601195317416)
XLA Ops:
  0.7 78.4 %shard_map.127 = bf16[128,8192]{1,0:T(8,128)(2,1)} custom-call(bf16[128,8192]{1,0:T(8,128)(2,1)} %input_hbm.1, bf16[64,128]{1,0:T(8,128)(2,1)} %bitcast.14, bf16[1024,128]{1,0:T(8,128)(2,1)} %qbase_hbm.1, bf16[64,1024]{1,0:T(8,128)(2,1)} %bitcast.10, bf16[64,128]{1,0:T(8,128)(2,1)} %qup_hbm.1, bf16[512,256]{1,0:T(8,128)(2,1)} %bitcast.8, ...), custom_call_target="tpu_custom_call" | custom-call | tf_op jit(solution)/shard_map/pallas_call | solution.py:613
  79.0 3.1 %copy.16 = bf16[128,8192]{1,0:T(8,128)(2,1)} copy(bf16[128,8192]{1,0:T(8,128)(2,1)} %shard_map.127) | data formatting | bytes 4194304
